TPU v7x, 32 devices: a whole 2x2x4 slice. The times are simulated.
32 devices in a mesh: groups: 2 (over y), ctx: 4 (over z), chan: 4 (over x, core).
Axes of the slice: x: 2, y: 2, z: 4, core: 2. Of those that a mesh axis runs over, the one named last changes fastest.
Arguments:
- q_feat: bfloat16 [4096, 8192], P(('groups', 'ctx'), 'chan'), parts along dimension 0, may hold values from -6 to 6
- k_feat: bfloat16 [4096, 8192], P(('groups', 'ctx'), 'chan'), parts along dimension 0, may hold values from -6 to 6
- v_feat: bfloat16 [4096, 8192], P(('groups', 'ctx'), 'chan'), parts along dimension 0, may hold values from -6 to 6
- pole_rate: float32 [16, 8192], P(None, 'chan'), may hold values from 4.8828126e-05 to 0.03
- residue: float32 [16, 8192], P(None, 'chan'), may hold values from -1.5 to 1.5
- skip_gain: float32 [8192], P('chan'), may hold values from 0.5 to 1.5
- lengths: int32 [8], P('groups'), parts along dimension 0, may hold values from 1 to 1024, 2048 in all
- owners: int32 [8], P('groups'), parts along dimension 0, may hold values from 0 to 3, as said below
Outputs:
- mixed_out: bfloat16 [4096, 8192], P(('groups', 'ctx'), 'chan'), parts along dimension 0
- decode_state: float32 [8, 16, 8192], P(('groups', 'ctx'), None, 'chan'), parts along dimension 0
There are 2 independent parts, one for each index of `groups`. A program takes and returns all parts, laid end to end along the dimension named above; an argument that names none is the same for every part. Nothing has to cross between parts.
Inputs may be any that keep to these rules, and one draw needn't show every extreme that they name: The 4 lengths sum to 2048; the longest is exactly 1024. The 4 owners are distinct.
All inputs are finite; a program needn't handle non-finite values.
Results may differ from a plain program's by a relative error of at most 0.001.
Values sent between devices are 32-bit elements; how exact they have to be, the bound alone decides.
No kernel may reach another device: no remote copies, remote signals or barrier semaphores. Data moves between devices by JAX's collectives and lax.ppermute only.
A program may use at most 128 MiB of HBM per device.

v0:
```python
import jax
import jax.numpy as jnp
from jax import lax
from jax.sharding import PartitionSpec as P

BLOCK = 32


HIGH = lax.Precision.HIGHEST


def from_behind(block, axis, distance):
    devices = range(lax.axis_size(axis))
    route = [(i - distance, i) for i in devices if i - distance in devices]
    return lax.ppermute(block, axis, route)


def shards(q_feat, k_feat, v_feat, pole_rate, residue, skip_gain, lengths, owners):
    tok_dev, channels = q_feat.shape
    pole_count = pole_rate.shape[0]
    request_count = lengths.shape[0]
    ctx_count = lax.axis_size("ctx")
    ctx_index = lax.axis_index("ctx")
    block_len = BLOCK
    block_count = tok_dev // block_len
    first_pos = ctx_index * tok_dev
    dev_last = first_pos + tok_dev - 1
    mixed_in = k_feat.astype(jnp.float32) * v_feat.astype(jnp.float32)
    offsets = jnp.cumsum(lengths) - lengths
    end_pos = offsets + lengths - 1
    positions = first_pos + jnp.arange(tok_dev, dtype=jnp.int32)
    segment = jnp.sum((positions[:, None] >= offsets[None, :]).astype(jnp.int32), axis=1) - 1
    before_seg = jnp.sum((first_pos - 1 >= offsets).astype(jnp.int32)) - 1
    last_seg = segment[tok_dev - 1]
    req_ids = jnp.arange(request_count, dtype=jnp.int32)
    scaled_res = residue * jnp.sqrt(1.0 - jnp.exp(-2.0 * pole_rate))
    step_float = jnp.arange(block_len, dtype=jnp.float32)
    decay_table = jnp.exp(-pole_rate[:, None, :] * step_float[None, :, None])
    decay_next = jnp.exp(-pole_rate[:, None, :] * (step_float[None, :, None] + 1.0))
    decay_back = decay_table[:, ::-1, :]
    block_decay = jnp.exp(-pole_rate * block_len)
    kernel = jnp.sum(scaled_res[:, None, :] * decay_table, axis=0)
    lag_steps = jnp.arange(block_len)[:, None] - jnp.arange(block_len)[None, :]
    toeplitz = jnp.where(
        (lag_steps >= 0)[:, :, None], kernel[jnp.clip(lag_steps, 0, block_len - 1)], 0.0
    )
    ref_pos = jnp.minimum(end_pos, dev_last)

    def block_step(loop_carry, block_inputs):
        mode_state, carry_seg, request_acc = loop_carry
        u_block, seg_block, block_index = block_inputs
        same_seg = (seg_block[:, None] == seg_block[None, :]).astype(jnp.float32)
        intra = jnp.einsum("ts,tsc,sc->tc", same_seg, toeplitz, u_block, precision=HIGH)
        live_mask = (seg_block == carry_seg).astype(jnp.float32)
        carried = (
            jnp.einsum("ptc,pc->tc", decay_next, scaled_res * mode_state, precision=HIGH)
            * live_mask[:, None]
        )
        seg_end = seg_block[block_len - 1]
        keep_mask = (carry_seg == seg_end).astype(jnp.float32)
        weighted = u_block * (seg_block == seg_end).astype(jnp.float32)[:, None]
        new_state = block_decay * mode_state * keep_mask + jnp.einsum(
            "psc,sc->pc", decay_back, weighted, precision=HIGH
        )
        block_end = first_pos + block_index * block_len + block_len - 1
        member = (seg_block[None, :] == req_ids[:, None]).astype(jnp.float32)
        collected = jnp.einsum("rs,psc,sc->rpc", member, decay_back, u_block, precision=HIGH)
        offset_steps = jnp.maximum(ref_pos - block_end, -(block_len - 1)).astype(jnp.float32)
        request_acc = (
            request_acc + jnp.exp(-pole_rate[None, :, :] * offset_steps[:, None, None]) * collected
        )
        return ((new_state, seg_end, request_acc), intra + carried)

    init_carry = (
        jnp.zeros((pole_count, channels), jnp.float32),
        before_seg,
        jnp.zeros((request_count, pole_count, channels), jnp.float32),
    )
    block_inputs = (
        mixed_in.reshape(block_count, block_len, channels),
        segment.reshape(block_count, block_len),
        jnp.arange(block_count, dtype=jnp.int32),
    )
    (local_end, seg_final, request_acc), local_out = lax.scan(block_step, init_carry, block_inputs)
    pass_mask = (last_seg == before_seg).astype(jnp.float32)
    span_decay = jnp.exp(-pole_rate * tok_dev) * pass_mask

    def relay_step(turn_index, incoming_now):
        outgoing = span_decay * incoming_now + local_end
        return from_behind(outgoing, "ctx", 1)

    incoming = lax.fori_loop(0, ctx_count - 1, relay_step, jnp.zeros_like(local_end))
    start_decay = jnp.exp(
        -pole_rate[None, :, :]
        * (jnp.arange(block_count, dtype=jnp.float32) * block_len)[:, None, None]
    )
    correction = jnp.einsum(
        "kpc,ptc->ktc",
        start_decay * (scaled_res * incoming)[None, :, :],
        decay_next,
        precision=HIGH,
    )
    live_dev = (segment == before_seg).astype(jnp.float32)
    conv = (
        local_out.reshape(tok_dev, channels)
        + correction.reshape(tok_dev, channels) * live_dev[:, None]
    )
    mixed_out = (q_feat.astype(jnp.float32) * (conv + skip_gain[None, :] * mixed_in)).astype(
        jnp.bfloat16
    )
    slot_ids = jnp.arange(ctx_count, dtype=jnp.int32)
    placement = (owners[None, :] == slot_ids[:, None]).astype(jnp.float32)
    ends_here = ((end_pos >= first_pos) & (end_pos <= dev_last)).astype(jnp.float32)
    from_before = (req_ids == before_seg).astype(jnp.float32)
    reach_steps = jnp.maximum(end_pos - first_pos + 1, 0).astype(jnp.float32)
    carried_in = jnp.exp(-pole_rate[None, :, :] * reach_steps[:, None, None]) * incoming[None, :, :]
    finished = (request_acc + from_before[:, None, None] * carried_in) * ends_here[:, None, None]
    slotted = jnp.einsum("qr,rpc->qpc", placement, finished, precision=HIGH)
    slotted = slotted.reshape(ctx_count, 1, pole_count, channels)
    received = lax.all_to_all(slotted, "ctx", split_axis=0, concat_axis=0, tiled=True)
    decode_state = jnp.sum(received, axis=0)
    return (mixed_out, decode_state)


def solution(mesh):
    placed = (
        P(("groups", "ctx"), "chan"),
        P(("groups", "ctx"), "chan"),
        P(("groups", "ctx"), "chan"),
        P(None, "chan"),
        P(None, "chan"),
        P("chan"),
        P("groups"),
        P("groups"),
    )
    return jax.shard_map(
        shards,
        mesh=mesh,
        in_specs=placed,
        out_specs=(P(("groups", "ctx"), "chan"), P(("groups", "ctx"), None, "chan")),
        check_vma=False,
    )
```

profile of v0, /device:TPU:0, one launch (start us, length us, event | category | flops | bytes accessed | tf_op | source)
XLA Modules:
  0.0 428.8 jit_solution(18111155510862013643)
XLA Ops:
  7.8 4.4 %multiply_reduce_fusion.2 = (f32[32,2048]{1,0:T(8,128)S(1)}, f32[16,32,2048]{2,1,0:T(8,128)}, f32[16,32,2048]{2,1,0:T(8,128)}) fusion(f32[16,2048]{1,0:T(8,128)S(1)} %get-tuple-element.641, f32[16,2048]{1,0:T(8,128)S(1)} %get-tuple-element.643, f32[32]{0:T(128)S(1)} %iota_add_fusion.1), kind=kLoop, calls=%fused_computation.47 | loop fusion | flops 4128768 | bytes 8913024 | tf_op jit(solution)/shard_map/reduce_sum | solution.py:42
  12.2 10.5 %rev.3 = f32[16,32,2048]{2,1,0:T(8,128)} reverse(f32[16,32,2048]{2,1,0:T(8,128)} %get-tuple-element.475), dimensions={1} | reverse | bytes 8388608 | tf_op jit(solution)/shard_map/rev | solution.py:40
  22.7 4.3 %convert_multiply_fusion = f32[512,2048]{1,0:T(8,128)} fusion(bf16[512,2048]{1,0:T(8,128)(2,1)S(1)} %copy-done.1, bf16[512,2048]{1,0:T(8,128)(2,1)} %param.13), kind=kLoop, calls=%fused_computation.49 | loop fusion | flops 3145728 | bytes 8388608 | tf_op jit(solution)/shard_map/mul | solution.py:28
  27.0 6.9 %gather_fusion = f32[1024,2048]{1,0:T(8,128)} fusion(f32[32,2048]{1,0:T(8,128)S(1)} %get-tuple-element.473, s32[1024]{0:T(1024)S(1)} %broadcast_clamp_fusion), kind=kCustom, calls=%fused_computation | custom fusion | bytes 16781312 | tf_op jit(solution)/shard_map/gather | solution.py:45
  33.9 7.3 %broadcast_select_fusion = f32[32,32,2048]{2,1,0:T(8,128)} fusion(f32[32,32,2048]{2,1,0:T(8,128)} %bitcast.125, pred[32,32]{1,0:T(8,128)(4,1)S(1)} %subtract_compare_fusion), kind=kLoop, calls=%fused_computation.46 | loop fusion | flops 2097152 | bytes 16778240 | tf_op jit(solution)/shard_map/jit(_where)/select_n | solution.py:44
  41.2 297.4 %while.32 = (s32[]{:T(128)}, f32[16,2048]{1,0:T(8,128)S(1)}, s32[]{:T(128)}, f32[4,16,2048]{2,0,1:T(4,128)S(1)}, f32[16,32,2048]{2,1,0:T(8,128)}, /*index=5*/f32...) while((s32[]{:T(128)}, f32[16,2048]{1,0:T(8,128)S(1)}, ...), condition=%wide.region_5.6_spmd.clone, body=%wide.region_4.5_spmd.clone.sunk | while | flops 84673808 | bytes 38801028 | solution.py:84
  45.8 2.9 multiply_reduce_fusion.5
  48.8 6.9 %fusion.66 = f32[32,1,2048]{2,1,0:T(1,128)S(1)} fusion(f32[32,32,2048]{2,1,0:T(8,128)} %get-tuple-element.682, f32[32,2048]{1,0:T(8,128)S(1)} %get-tuple-element.624, pred[32,32,1]{1,0,2:T(32,128)(4,1)S(1)} %compare_bitcast_fusion.2), kind=kOutput, calls=%fused_computation.4.clone.1 | convolution fusion | flops 27262976 | bytes 8913920 | tf_op jit(solution)/shard_map/while/body/eval_jaxpr/ts,tsc,sc->tc/dot_general | solution.py:53
  67.3 6.9 %fusion.66 = f32[32,1,2048]{2,1,0:T(1,128)S(1)} fusion(f32[32,32,2048]{2,1,0:T(8,128)} %get-tuple-element.682, f32[32,2048]{1,0:T(8,128)S(1)} %get-tuple-element.624, pred[32,32,1]{1,0,2:T(32,128)(4,1)S(1)} %compare_bitcast_fusion.2), kind=kOutput, calls=%fused_computation.4.clone.1 | convolution fusion | flops 27262976 | bytes 8913920 | tf_op jit(solution)/shard_map/while/body/eval_jaxpr/ts,tsc,sc->tc/dot_general | solution.py:53
  85.9 6.9 %fusion.66 = f32[32,1,2048]{2,1,0:T(1,128)S(1)} fusion(f32[32,32,2048]{2,1,0:T(8,128)} %get-tuple-element.682, f32[32,2048]{1,0:T(8,128)S(1)} %get-tuple-element.624, pred[32,32,1]{1,0,2:T(32,128)(4,1)S(1)} %compare_bitcast_fusion.2), kind=kOutput, calls=%fused_computation.4.clone.1 | convolution fusion | flops 27262976 | bytes 8913920 | tf_op jit(solution)/shard_map/while/body/eval_jaxpr/ts,tsc,sc->tc/dot_general | solution.py:53
  104.5 6.9 %fusion.66 = f32[32,1,2048]{2,1,0:T(1,128)S(1)} fusion(f32[32,32,2048]{2,1,0:T(8,128)} %get-tuple-element.682, f32[32,2048]{1,0:T(8,128)S(1)} %get-tuple-element.624, pred[32,32,1]{1,0,2:T(32,128)(4,1)S(1)} %compare_bitcast_fusion.2), kind=kOutput, calls=%fused_computation.4.clone.1 | convolution fusion | flops 27262976 | bytes 8913920 | tf_op jit(solution)/shard_map/while/body/eval_jaxpr/ts,tsc,sc->tc/dot_general | solution.py:53
  123.1 6.9 %fusion.66 = f32[32,1,2048]{2,1,0:T(1,128)S(1)} fusion(f32[32,32,2048]{2,1,0:T(8,128)} %get-tuple-element.682, f32[32,2048]{1,0:T(8,128)S(1)} %get-tuple-element.624, pred[32,32,1]{1,0,2:T(32,128)(4,1)S(1)} %compare_bitcast_fusion.2), kind=kOutput, calls=%fused_computation.4.clone.1 | convolution fusion | flops 27262976 | bytes 8913920 | tf_op jit(solution)/shard_map/while/body/eval_jaxpr/ts,tsc,sc->tc/dot_general | solution.py:53
  141.7 6.9 %fusion.66 = f32[32,1,2048]{2,1,0:T(1,128)S(1)} fusion(f32[32,32,2048]{2,1,0:T(8,128)} %get-tuple-element.682, f32[32,2048]{1,0:T(8,128)S(1)} %get-tuple-element.624, pred[32,32,1]{1,0,2:T(32,128)(4,1)S(1)} %compare_bitcast_fusion.2), kind=kOutput, calls=%fused_computation.4.clone.1 | convolution fusion | flops 27262976 | bytes 8913920 | tf_op jit(solution)/shard_map/while/body/eval_jaxpr/ts,tsc,sc->tc/dot_general | solution.py:53
  160.3 6.9 %fusion.66 = f32[32,1,2048]{2,1,0:T(1,128)S(1)} fusion(f32[32,32,2048]{2,1,0:T(8,128)} %get-tuple-element.682, f32[32,2048]{1,0:T(8,128)S(1)} %get-tuple-element.624, pred[32,32,1]{1,0,2:T(32,128)(4,1)S(1)} %compare_bitcast_fusion.2), kind=kOutput, calls=%fused_computation.4.clone.1 | convolution fusion | flops 27262976 | bytes 8913920 | tf_op jit(solution)/shard_map/while/body/eval_jaxpr/ts,tsc,sc->tc/dot_general | solution.py:53
  178.9 6.9 %fusion.66 = f32[32,1,2048]{2,1,0:T(1,128)S(1)} fusion(f32[32,32,2048]{2,1,0:T(8,128)} %get-tuple-element.682, f32[32,2048]{1,0:T(8,128)S(1)} %get-tuple-element.624, pred[32,32,1]{1,0,2:T(32,128)(4,1)S(1)} %compare_bitcast_fusion.2), kind=kOutput, calls=%fused_computation.4.clone.1 | convolution fusion | flops 27262976 | bytes 8913920 | tf_op jit(solution)/shard_map/while/body/eval_jaxpr/ts,tsc,sc->tc/dot_general | solution.py:53
  197.4 6.9 %fusion.66 = f32[32,1,2048]{2,1,0:T(1,128)S(1)} fusion(f32[32,32,2048]{2,1,0:T(8,128)} %get-tuple-element.682, f32[32,2048]{1,0:T(8,128)S(1)} %get-tuple-element.624, pred[32,32,1]{1,0,2:T(32,128)(4,1)S(1)} %compare_bitcast_fusion.2), kind=kOutput, calls=%fused_computation.4.clone.1 | convolution fusion | flops 27262976 | bytes 8913920 | tf_op jit(solution)/shard_map/while/body/eval_jaxpr/ts,tsc,sc->tc/dot_general | solution.py:53
  216.0 6.9 %fusion.66 = f32[32,1,2048]{2,1,0:T(1,128)S(1)} fusion(f32[32,32,2048]{2,1,0:T(8,128)} %get-tuple-element.682, f32[32,2048]{1,0:T(8,128)S(1)} %get-tuple-element.624, pred[32,32,1]{1,0,2:T(32,128)(4,1)S(1)} %compare_bitcast_fusion.2), kind=kOutput, calls=%fused_computation.4.clone.1 | convolution fusion | flops 27262976 | bytes 8913920 | tf_op jit(solution)/shard_map/while/body/eval_jaxpr/ts,tsc,sc->tc/dot_general | solution.py:53
  234.6 6.9 %fusion.66 = f32[32,1,2048]{2,1,0:T(1,128)S(1)} fusion(f32[32,32,2048]{2,1,0:T(8,128)} %get-tuple-element.682, f32[32,2048]{1,0:T(8,128)S(1)} %get-tuple-element.624, pred[32,32,1]{1,0,2:T(32,128)(4,1)S(1)} %compare_bitcast_fusion.2), kind=kOutput, calls=%fused_computation.4.clone.1 | convolution fusion | flops 27262976 | bytes 8913920 | tf_op jit(solution)/shard_map/while/body/eval_jaxpr/ts,tsc,sc->tc/dot_general | solution.py:53
  253.2 6.9 %fusion.66 = f32[32,1,2048]{2,1,0:T(1,128)S(1)} fusion(f32[32,32,2048]{2,1,0:T(8,128)} %get-tuple-element.682, f32[32,2048]{1,0:T(8,128)S(1)} %get-tuple-element.624, pred[32,32,1]{1,0,2:T(32,128)(4,1)S(1)} %compare_bitcast_fusion.2), kind=kOutput, calls=%fused_computation.4.clone.1 | convolution fusion | flops 27262976 | bytes 8913920 | tf_op jit(solution)/shard_map/while/body/eval_jaxpr/ts,tsc,sc->tc/dot_general | solution.py:53
  271.8 6.9 %fusion.66 = f32[32,1,2048]{2,1,0:T(1,128)S(1)} fusion(f32[32,32,2048]{2,1,0:T(8,128)} %get-tuple-element.682, f32[32,2048]{1,0:T(8,128)S(1)} %get-tuple-element.624, pred[32,32,1]{1,0,2:T(32,128)(4,1)S(1)} %compare_bitcast_fusion.2), kind=kOutput, calls=%fused_computation.4.clone.1 | convolution fusion | flops 27262976 | bytes 8913920 | tf_op jit(solution)/shard_map/while/body/eval_jaxpr/ts,tsc,sc->tc/dot_general | solution.py:53
  290.4 6.9 %fusion.66 = f32[32,1,2048]{2,1,0:T(1,128)S(1)} fusion(f32[32,32,2048]{2,1,0:T(8,128)} %get-tuple-element.682, f32[32,2048]{1,0:T(8,128)S(1)} %get-tuple-element.624, pred[32,32,1]{1,0,2:T(32,128)(4,1)S(1)} %compare_bitcast_fusion.2), kind=kOutput, calls=%fused_computation.4.clone.1 | convolution fusion | flops 27262976 | bytes 8913920 | tf_op jit(solution)/shard_map/while/body/eval_jaxpr/ts,tsc,sc->tc/dot_general | solution.py:53
  309.0 6.9 %fusion.66 = f32[32,1,2048]{2,1,0:T(1,128)S(1)} fusion(f32[32,32,2048]{2,1,0:T(8,128)} %get-tuple-element.682, f32[32,2048]{1,0:T(8,128)S(1)} %get-tuple-element.624, pred[32,32,1]{1,0,2:T(32,128)(4,1)S(1)} %compare_bitcast_fusion.2), kind=kOutput, calls=%fused_computation.4.clone.1 | convolution fusion | flops 27262976 | bytes 8913920 | tf_op jit(solution)/shard_map/while/body/eval_jaxpr/ts,tsc,sc->tc/dot_general | solution.py:53
  327.5 6.9 %fusion.66 = f32[32,1,2048]{2,1,0:T(1,128)S(1)} fusion(f32[32,32,2048]{2,1,0:T(8,128)} %get-tuple-element.682, f32[32,2048]{1,0:T(8,128)S(1)} %get-tuple-element.624, pred[32,32,1]{1,0,2:T(32,128)(4,1)S(1)} %compare_bitcast_fusion.2), kind=kOutput, calls=%fused_computation.4.clone.1 | convolution fusion | flops 27262976 | bytes 8913920 | tf_op jit(solution)/shard_map/while/body/eval_jaxpr/ts,tsc,sc->tc/dot_general | solution.py:53
  338.6 21.5 %while.31 = (s32[]{:T(128)}, f32[16,2048]{1,0:T(8,128)S(1)}, f32[16,2048]{1,0:T(8,128)S(1)}, f32[16,2048]{1,0:T(8,128)S(1)}, s32[]{:T(128)}) while((s32[]{:T(128)}, f32[16,2048]{1,0:T(8,128)S(1)}, f32[16,2048]{1,0:T(8,128)S(1)}, f32[16,2048]{1,0:T(8,128)S(1)}, s32[]{:T(128)}) %tuple.78), condition=%wide.region_7.8_spmd, body=%wide.region_6.7_spmd.sunk | while | flops 65538 | bytes 1048677 | solution.py:92
  338.6 4.9 %collective-permute-start = (f32[16,2048]{1,0:T(8,128)S(1)}, f32[16,2048]{1,0:T(8,128)S(1)}, u32[]{:S(2)}, u32[]{:S(2)}) collective-permute-start(f32[16,2048]{1,0:T(8,128)S(1)} %multiply_add_fusion.2), channel_id=1, source_target_pairs={{0,4},{4,8},{8,12},{1,5},{5,9},{9,13},{2,6},{6,10},{10,14},{3,7},{... | collective-permute-start | bytes 393224 | tf_op jit(solution)/shard_map/while/body/eval_jaxpr/ppermute | solution.py:15
  346.3 4.4 %collective-permute-start = (f32[16,2048]{1,0:T(8,128)S(1)}, f32[16,2048]{1,0:T(8,128)S(1)}, u32[]{:S(2)}, u32[]{:S(2)}) collective-permute-start(f32[16,2048]{1,0:T(8,128)S(1)} %multiply_add_fusion.2), channel_id=1, source_target_pairs={{0,4},{4,8},{8,12},{1,5},{5,9},{9,13},{2,6},{6,10},{10,14},{3,7},{... | collective-permute-start | bytes 393224 | tf_op jit(solution)/shard_map/while/body/eval_jaxpr/ppermute | solution.py:15
  353.2 4.4 %collective-permute-start = (f32[16,2048]{1,0:T(8,128)S(1)}, f32[16,2048]{1,0:T(8,128)S(1)}, u32[]{:S(2)}, u32[]{:S(2)}) collective-permute-start(f32[16,2048]{1,0:T(8,128)S(1)} %multiply_add_fusion.2), channel_id=1, source_target_pairs={{0,4},{4,8},{8,12},{1,5},{5,9},{9,13},{2,6},{6,10},{10,14},{3,7},{... | collective-permute-start | bytes 393224 | tf_op jit(solution)/shard_map/while/body/eval_jaxpr/ppermute | solution.py:15
  363.1 5.7 %all-to-all-start = ((f32[4,1,16,2048]{3,2,1,0:T(8,128)}), f32[4,1,16,2048]{3,2,1,0:T(8,128)}, u32[]{:S(2)}, u32[]{:S(2)}) async-start(f32[4,1,16,2048]{3,2,1,0:T(8,128)} %copy.27), calls=%async_computation | async-start | bytes 1048576 | tf_op jit(solution)/shard_map/all_to_all | solution.py:120
  371.5 12.6 %copy.25 = f32[16,32,2048]{1,0,2:T(8,128)} copy(f32[16,32,2048]{2,1,0:T(8,128)} %get-tuple-element.474) | data formatting | bytes 8388608 | tf_op jit(solution)/shard_map/exp | solution.py:39
  384.1 23.6 %fusion.29 = f32[16,32,2048]{1,0,2:T(8,128)} fusion(f32[16,32,2048]{1,0,2:T(8,128)} %copy.25, f32[16,2048]{0,1:T(8,128)} %copy.24, f32[16]{0:T(128)S(1)} %iota_multiply_fusion, f32[16,2048]{0,1:T(8,128)S(1)} %copy-done.2), kind=kOutput, calls=%fused_computation.36 | convolution fusion | flops 202375168 | bytes 8650816 | tf_op jit(solution)/shard_map/kpc,ptc->ktc/dot_general | solution.py:97
  407.7 11.5 %copy.26 = f32[16,32,2048]{2,1,0:T(8,128)} copy(f32[16,32,2048]{1,0,2:T(8,128)} %fusion.29) | data formatting | bytes 8388608 | tf_op jit(solution)/shard_map/kpc,ptc->ktc/transpose | solution.py:97
  419.2 7.8 %fusion.38 = bf16[512,2048]{1,0:T(8,128)(2,1)} fusion(f32[16,32,2048]{2,1,0:T(8,128)} %copy.26, f32[16,32,2048]{2,1,0:T(8,128)} %get-tuple-element.359, bf16[512,2048]{1,0:T(8,128)(2,1)} %param.12, f32[2048]{0:T(1024)S(1)} %copy-done.6, f32[512]{0:T(512)S(1)} %compare_convert_fusion.3, bf16[512,2048]{1,0:T(8,128)(2,1)S(1)} %copy-done.1, ...), kind=kLoop, calls=%fused_computation.44 | loop fusion | flops 10485760 | bytes 16787456 | tf_op jit(solution)/shard_map/convert_element_type | solution.py:108
  (273 shorter events, 178.0 us)
Async XLA Ops:
  7.8 4.5 %copy-start.3 = (f32[16,2048]{1,0:T(8,128)}, f32[16,2048]{1,0:T(8,128)S(1)}, u32[]{:S(2)}) copy-start(f32[16,2048]{1,0:T(8,128)S(1)} %get-tuple-element.643) | copy-start | bytes 393220
  12.2 10.5 %copy-start.1 = (bf16[512,2048]{1,0:T(8,128)(2,1)S(1)}, bf16[512,2048]{1,0:T(8,128)(2,1)}, u32[]{:S(2)}) copy-start(bf16[512,2048]{1,0:T(8,128)(2,1)} %param.14) | copy-start | bytes 6291460
  33.9 7.3 %copy-start.4 = (f32[16,2048]{1,0:T(8,128)S(1)}, f32[16,2048]{1,0:T(8,128)}, u32[]{:S(2)}) copy-start(f32[16,2048]{1,0:T(8,128)} %copy-done.3) | copy-start | bytes 393220
  33.9 7.3 %copy-start.8 = (s32[4]{0:T(128)S(1)}, s32[4]{0:T(128)}, u32[]{:S(2)}) copy-start(s32[4]{0:T(128)} %get-tuple-element.639) | copy-start | bytes 52
  41.1 318.9 %copy-start.7 = (f32[4]{0:T(128)S(1)}, f32[4]{0:T(128)}, u32[]{:S(2)}) copy-start(f32[4]{0:T(128)} %get-tuple-element.481) | copy-start | bytes 52
  48.7 6.9 %copy-start = (f32[16,32,2048]{2,1,0:T(8,128)S(1)}, f32[16,32,2048]{2,1,0:T(8,128)}, u32[]{:S(2)}) copy-start(f32[16,32,2048]{2,1,0:T(8,128)} %get-tuple-element.677) | copy-start | bytes 12582916 | tf_op jit(solution)/shard_map/while
  67.3 6.9 %copy-start = (f32[16,32,2048]{2,1,0:T(8,128)S(1)}, f32[16,32,2048]{2,1,0:T(8,128)}, u32[]{:S(2)}) copy-start(f32[16,32,2048]{2,1,0:T(8,128)} %get-tuple-element.677) | copy-start | bytes 12582916 | tf_op jit(solution)/shard_map/while
  85.9 6.9 %copy-start = (f32[16,32,2048]{2,1,0:T(8,128)S(1)}, f32[16,32,2048]{2,1,0:T(8,128)}, u32[]{:S(2)}) copy-start(f32[16,32,2048]{2,1,0:T(8,128)} %get-tuple-element.677) | copy-start | bytes 12582916 | tf_op jit(solution)/shard_map/while
  104.5 6.9 %copy-start = (f32[16,32,2048]{2,1,0:T(8,128)S(1)}, f32[16,32,2048]{2,1,0:T(8,128)}, u32[]{:S(2)}) copy-start(f32[16,32,2048]{2,1,0:T(8,128)} %get-tuple-element.677) | copy-start | bytes 12582916 | tf_op jit(solution)/shard_map/while
  123.1 6.9 %copy-start = (f32[16,32,2048]{2,1,0:T(8,128)S(1)}, f32[16,32,2048]{2,1,0:T(8,128)}, u32[]{:S(2)}) copy-start(f32[16,32,2048]{2,1,0:T(8,128)} %get-tuple-element.677) | copy-start | bytes 12582916 | tf_op jit(solution)/shard_map/while
  141.7 6.9 %copy-start = (f32[16,32,2048]{2,1,0:T(8,128)S(1)}, f32[16,32,2048]{2,1,0:T(8,128)}, u32[]{:S(2)}) copy-start(f32[16,32,2048]{2,1,0:T(8,128)} %get-tuple-element.677) | copy-start | bytes 12582916 | tf_op jit(solution)/shard_map/while
  160.3 6.9 %copy-start = (f32[16,32,2048]{2,1,0:T(8,128)S(1)}, f32[16,32,2048]{2,1,0:T(8,128)}, u32[]{:S(2)}) copy-start(f32[16,32,2048]{2,1,0:T(8,128)} %get-tuple-element.677) | copy-start | bytes 12582916 | tf_op jit(solution)/shard_map/while
  178.8 6.9 %copy-start = (f32[16,32,2048]{2,1,0:T(8,128)S(1)}, f32[16,32,2048]{2,1,0:T(8,128)}, u32[]{:S(2)}) copy-start(f32[16,32,2048]{2,1,0:T(8,128)} %get-tuple-element.677) | copy-start | bytes 12582916 | tf_op jit(solution)/shard_map/while
  197.4 6.9 %copy-start = (f32[16,32,2048]{2,1,0:T(8,128)S(1)}, f32[16,32,2048]{2,1,0:T(8,128)}, u32[]{:S(2)}) copy-start(f32[16,32,2048]{2,1,0:T(8,128)} %get-tuple-element.677) | copy-start | bytes 12582916 | tf_op jit(solution)/shard_map/while
  216.0 6.9 %copy-start = (f32[16,32,2048]{2,1,0:T(8,128)S(1)}, f32[16,32,2048]{2,1,0:T(8,128)}, u32[]{:S(2)}) copy-start(f32[16,32,2048]{2,1,0:T(8,128)} %get-tuple-element.677) | copy-start | bytes 12582916 | tf_op jit(solution)/shard_map/while
  234.6 6.9 %copy-start = (f32[16,32,2048]{2,1,0:T(8,128)S(1)}, f32[16,32,2048]{2,1,0:T(8,128)}, u32[]{:S(2)}) copy-start(f32[16,32,2048]{2,1,0:T(8,128)} %get-tuple-element.677) | copy-start | bytes 12582916 | tf_op jit(solution)/shard_map/while
  253.2 6.9 %copy-start = (f32[16,32,2048]{2,1,0:T(8,128)S(1)}, f32[16,32,2048]{2,1,0:T(8,128)}, u32[]{:S(2)}) copy-start(f32[16,32,2048]{2,1,0:T(8,128)} %get-tuple-element.677) | copy-start | bytes 12582916 | tf_op jit(solution)/shard_map/while
  271.8 6.9 %copy-start = (f32[16,32,2048]{2,1,0:T(8,128)S(1)}, f32[16,32,2048]{2,1,0:T(8,128)}, u32[]{:S(2)}) copy-start(f32[16,32,2048]{2,1,0:T(8,128)} %get-tuple-element.677) | copy-start | bytes 12582916 | tf_op jit(solution)/shard_map/while
  290.4 6.9 %copy-start = (f32[16,32,2048]{2,1,0:T(8,128)S(1)}, f32[16,32,2048]{2,1,0:T(8,128)}, u32[]{:S(2)}) copy-start(f32[16,32,2048]{2,1,0:T(8,128)} %get-tuple-element.677) | copy-start | bytes 12582916 | tf_op jit(solution)/shard_map/while
  308.9 6.9 %copy-start = (f32[16,32,2048]{2,1,0:T(8,128)S(1)}, f32[16,32,2048]{2,1,0:T(8,128)}, u32[]{:S(2)}) copy-start(f32[16,32,2048]{2,1,0:T(8,128)} %get-tuple-element.677) | copy-start | bytes 12582916 | tf_op jit(solution)/shard_map/while
  327.5 6.9 %copy-start = (f32[16,32,2048]{2,1,0:T(8,128)S(1)}, f32[16,32,2048]{2,1,0:T(8,128)}, u32[]{:S(2)}) copy-start(f32[16,32,2048]{2,1,0:T(8,128)} %get-tuple-element.677) | copy-start | bytes 12582916 | tf_op jit(solution)/shard_map/while
  338.5 30.3 %copy-start.5 = (f32[16,2048]{1,0:T(8,128)S(1)}, f32[16,2048]{1,0:T(8,128)}, u32[]{:S(2)}) copy-start(f32[16,2048]{1,0:T(8,128)} %copy-done.3) | copy-start | bytes 393220
  338.6 7.7 %collective-permute-start = (f32[16,2048]{1,0:T(8,128)S(1)}, f32[16,2048]{1,0:T(8,128)S(1)}, u32[]{:S(2)}, u32[]{:S(2)}) collective-permute-start(f32[16,2048]{1,0:T(8,128)S(1)} %multiply_add_fusion.2), channel_id=1, source_target_pairs={{0,4},{4,8},{8,12},{1,5},{5,9},{9,13},{2,6},{6,10},{10,14},{3,7},{... | collective-permute-start | bytes 393224 | tf_op jit(solution)/shard_map/while/body/eval_jaxpr/ppermute | solution.py:15
  346.3 6.9 %collective-permute-start = (f32[16,2048]{1,0:T(8,128)S(1)}, f32[16,2048]{1,0:T(8,128)S(1)}, u32[]{:S(2)}, u32[]{:S(2)}) collective-permute-start(f32[16,2048]{1,0:T(8,128)S(1)} %multiply_add_fusion.2), channel_id=1, source_target_pairs={{0,4},{4,8},{8,12},{1,5},{5,9},{9,13},{2,6},{6,10},{10,14},{3,7},{... | collective-permute-start | bytes 393224 | tf_op jit(solution)/shard_map/while/body/eval_jaxpr/ppermute | solution.py:15
  353.2 6.9 %collective-permute-start = (f32[16,2048]{1,0:T(8,128)S(1)}, f32[16,2048]{1,0:T(8,128)S(1)}, u32[]{:S(2)}, u32[]{:S(2)}) collective-permute-start(f32[16,2048]{1,0:T(8,128)S(1)} %multiply_add_fusion.2), channel_id=1, source_target_pairs={{0,4},{4,8},{8,12},{1,5},{5,9},{9,13},{2,6},{6,10},{10,14},{3,7},{... | collective-permute-start | bytes 393224 | tf_op jit(solution)/shard_map/while/body/eval_jaxpr/ppermute | solution.py:15
  363.1 64.0 %all-to-all-start = ((f32[4,1,16,2048]{3,2,1,0:T(8,128)}), f32[4,1,16,2048]{3,2,1,0:T(8,128)}, u32[]{:S(2)}, u32[]{:S(2)}) async-start(f32[4,1,16,2048]{3,2,1,0:T(8,128)} %copy.27), calls=%async_computation | async-start | bytes 1048576 | tf_op jit(solution)/shard_map/all_to_all | solution.py:120
  371.5 12.6 %copy-start.2 = (f32[16,2048]{0,1:T(8,128)S(1)}, f32[16,2048]{0,1:T(8,128)}, u32[]{:S(2)}) copy-start(f32[16,2048]{0,1:T(8,128)} %copy.23) | copy-start | bytes 393220
  407.7 11.5 %copy-start.6 = (f32[2048]{0:T(1024)S(1)}, f32[2048]{0:T(1024)}, u32[]{:S(2)}) copy-start(f32[2048]{0:T(1024)} %param.17) | copy-start | bytes 24580
where the time goes:
time: 432 us; the launch traced here: 429 us
  matrix products  167 us (39%)
  other arithmetic  141 us (33%)
  local copies, waits for them, and re-layouts  64.3 us (15%)
  loops' own time  27.7 us (6%)
  starting transfers between devices  19.4 us (4%)
  waiting for transfers between devices  7.71 us (2%)
    dot_general x16, matrix products, block_step(): jnp.einsum('ts,tsc,sc->tc', same_seg, toeplitz, u_block, precision=HIGH)  110 us
    dot_general x16, other arithmetic, block_step(): jnp.einsum('psc,sc->pc', decay_back, weighted, precision=HIGH)  46.1 us
    dot_general x16, matrix products, block_step(): jnp.einsum('rs,psc,sc->rpc', member, decay_back, u_block, precision=HIGH)  31.5 us
    another operation x1, loops' own time, shards(): lax.scan(block_step, init_carry, block_inputs)  27.6 us
    dot_general x1, matrix products, shards(): jnp.einsum('kpc,ptc->ktc', start_decay * (scaled_res * incoming)[None, :,...  23.6 us
    while x32, other arithmetic  18 us
    ppermute x3, starting transfers between devices, from_behind(): return lax.ppermute(block, axis, route)  13.7 us
    dynamic_update_slice x16, other arithmetic, shards(): lax.scan(block_step, init_carry, block_inputs)  13.3 us
  transfers between devices with their start and end apart: 4, of which 3 were waited for; matrix products, arithmetic and copies ran while one was open for 14% of the time, Pallas kernels for 0%

commit v1 on v0

v1 whole, which is shorter than its diff:
```python
import functools

import jax
import jax.numpy as jnp
from jax import lax
from jax.experimental import pallas as pl
from jax.experimental.pallas import tpu as pltpu
from jax.sharding import PartitionSpec as P

LANES = 128
SUBS = 8
CHUNK = 64
UNROLL = 8
VMEM_BYTES = 40 * 1024 * 1024


def request_span(lengths_ref, request, request_count):
    start = jnp.int32(0)
    length = jnp.int32(0)
    for r in range(request_count):
        start = start + jnp.where(r < request, lengths_ref[r], 0)
        length = length + jnp.where(r == request, lengths_ref[r], 0)
    return start, start + length - 1


def request_at(lengths_ref, position, request_count):
    index = jnp.int32(-1)
    start = jnp.int32(0)
    for r in range(request_count):
        index = index + (start <= position).astype(jnp.int32)
        start = start + lengths_ref[r]
    return index


def token_loop(lo, hi, step, carry):
    count = jnp.maximum(hi - lo, 0)
    groups = lax.div(count, jnp.int32(UNROLL))

    def many(g, carry):
        base = lo + g * UNROLL
        for s in range(UNROLL):
            carry = step(base + s, carry)
        return carry

    carry = lax.fori_loop(0, groups, many, carry)
    return lax.fori_loop(lo + groups * UNROLL, lo + count, step, carry)


def to_rows(value_ref, rows_ref, tiles, change=lambda x: x):
    pole_count = value_ref.shape[0]
    span = max(tiles, SUBS)
    for pt in range(pole_count // SUBS):
        for j in range(tiles):
            tile = value_ref[pt * SUBS : (pt + 1) * SUBS, j * LANES : (j + 1) * LANES]
            rows_ref[pl.ds(pt * SUBS * span + j, SUBS, stride=span), :] = change(tile)


def chunk_copies(pairs, sems, c):
    rows = pl.ds(pl.multiple_of(c * CHUNK, CHUNK), CHUNK)
    return [
        pltpu.make_async_copy(src.at[rows, :], dst.at[rows, :], sems.at[n, c])
        for n, (src, dst) in enumerate(pairs)
    ]


def fill_rows(k_buf, v_buf, u_rows, c, tiles):
    span = max(tiles, SUBS)

    def block(b, _):
        rows = pl.ds(pl.multiple_of(c * CHUNK + b * 16, 16), 16)
        for j in range(tiles):
            lanes = slice(j * LANES, (j + 1) * LANES)
            u = k_buf[rows, lanes].astype(jnp.float32) * v_buf[rows, lanes].astype(jnp.float32)
            for half in range(2):
                u_rows[pl.ds((b * 16 + half * SUBS) * span + j, SUBS, stride=span), :] = u[
                    half * SUBS : (half + 1) * SUBS
                ]
        return 0

    lax.fori_loop(0, CHUNK // 16, block, 0)


def row_at(row, h, span):
    return pl.ds(pl.multiple_of(row * span + h * SUBS, SUBS), SUBS)


def row_tile(ref, row, h, span):
    return ref[row_at(row, h, span), :]


def pieces_kernel(
    request_count, lengths_ref, owners_ref, k_hbm, v_hbm, rate_ref, *rest
):
    n = lax.axis_size("ctx")
    i = lax.axis_index("ctx")
    far_count = n - 3
    even_ref, odd_ref, next_ref, own_ref = rest[:4]
    far_refs = rest[4 : 4 + far_count]
    k_buf, v_buf, u_rows, a_rows, states, sems = rest[4 + far_count :]
    pole_count, channels = rate_ref.shape
    tok_dev = k_buf.shape[0]
    tiles = channels // LANES
    span = max(tiles, SUBS)
    halves = span // SUBS
    chunks = tok_dev // CHUNK
    first = i * tok_dev
    last = first + tok_dev - 1
    moves = ((k_hbm, k_buf), (v_hbm, v_buf))
    for c in range(chunks):
        for copy in chunk_copies(moves, sems, c):
            copy.start()
    to_rows(rate_ref, a_rows, tiles, lambda x: jnp.exp(-x))

    def clear(b, _):
        states[pl.ds(pl.multiple_of(b * SUBS, SUBS), SUBS), :] = jnp.zeros((SUBS, LANES), jnp.float32)
        return 0

    lax.fori_loop(0, request_count * pole_count * halves, clear, 0)

    def chunk(c, _):
        for copy in chunk_copies(moves, sems, c):
            copy.wait()
        fill_rows(k_buf, v_buf, u_rows, c, tiles)
        base = first + c * CHUNK

        def request(r, start):
            length = lengths_ref[r]
            lo = jnp.maximum(start - base, 0)
            hi = jnp.minimum(start + length - base, CHUNK)

            @pl.when(hi > lo)
            def _():
                def half(h, _):
                    decay = [row_tile(a_rows, p, h, span) for p in range(pole_count)]
                    state = tuple(
                        row_tile(states, r * pole_count + p, h, span) for p in range(pole_count)
                    )

                    def step(t, state):
                        u = row_tile(u_rows, t, h, span)
                        return tuple(s * a + u for s, a in zip(state, decay))

                    state = token_loop(lo, hi, step, state)
                    for p in range(pole_count):
                        states[row_at(r * pole_count + p, h, span), :] = state[p]
                    return 0

                lax.fori_loop(0, halves, half, 0)

            return start + length

        lax.fori_loop(0, request_count, request, jnp.int32(0))
        return 0

    lax.fori_loop(0, chunks, chunk, 0)

    def owned(slot):
        request = jnp.int32(0)
        found = jnp.int32(0)
        for r in range(request_count):
            match = (owners_ref[r] == slot).astype(jnp.int32)
            request = request + r * match
            found = found + match
        start, end = request_span(lengths_ref, request, request_count)
        live = (found > 0) & (start <= last) & (end >= first)
        return request, jnp.maximum(end - last, 0), live

    def emit(out_ref, what):
        request, steps, live = what
        rate_scale = -steps.astype(jnp.float32)
        keep = jnp.where(live, 1.0, 0.0).astype(jnp.float32)
        for pt in range(pole_count // SUBS):
            for j in range(tiles):
                rows = slice(pt * SUBS, (pt + 1) * SUBS)
                lanes = slice(j * LANES, (j + 1) * LANES)
                state = states[
                    pl.ds((request * pole_count + pt * SUBS) * span + j, SUBS, stride=span), :
                ]
                out_ref[rows, lanes] = state * (jnp.exp(rate_ref[rows, lanes] * rate_scale) * keep)

    def pick(flag, yes, no):
        return tuple(jnp.where(flag, a, b) for a, b in zip(yes, no))

    odd = lax.rem(i, 2) == 1
    crossing = (request_at(lengths_ref, last, request_count), jnp.int32(0), jnp.bool_(True))
    behind = owned(lax.rem(i + n - 1, n))
    ahead = owned(lax.rem(i + 1, n))
    emit(even_ref, pick(odd, behind, crossing))
    odd_forward = pick(i == n - 1, ahead, crossing)
    emit(odd_ref, pick(odd, odd_forward, behind))
    for d, far_ref in enumerate(far_refs):
        emit(far_ref, owned(lax.rem(i + 2 + d, n)))
    emit(next_ref, ahead)
    emit(own_ref, owned(i))


def local_kernel(
    request_count,
    lengths_ref,
    k_hbm,
    v_hbm,
    rate_ref,
    residue_ref,
    skip_ref,
    out_hbm,
    k_buf,
    v_buf,
    out_buf,
    u_rows,
    y_rows,
    a_rows,
    r_rows,
    states,
    sems,
    out_sems,
):
    i = lax.axis_index("ctx")
    pole_count, channels = rate_ref.shape
    tok_dev = k_buf.shape[0]
    tiles = channels // LANES
    span = max(tiles, SUBS)
    halves = span // SUBS
    chunks = tok_dev // CHUNK
    first = i * tok_dev
    moves = ((k_hbm, k_buf), (v_hbm, v_buf))
    for c in range(chunks):
        for copy in chunk_copies(moves, sems, c):
            copy.start()
    to_rows(rate_ref, a_rows, tiles, lambda x: jnp.exp(-x))
    scaled_rows(rate_ref, residue_ref, r_rows, tiles)

    def chunk(c, _):
        for copy in chunk_copies(moves, sems, c):
            copy.wait()
        fill_rows(k_buf, v_buf, u_rows, c, tiles)
        base = first + c * CHUNK

        def request(r, start):
            length = lengths_ref[r]
            lo = jnp.maximum(start - base, 0)
            hi = jnp.minimum(start + length - base, CHUNK)

            @pl.when(hi > lo)
            def _():
                fresh = (start >= base) | (c == 0)

                def half(h, _):
                    decay = [row_tile(a_rows, p, h, span) for p in range(pole_count)]
                    gain = [row_tile(r_rows, p, h, span) for p in range(pole_count)]
                    state = tuple(
                        jnp.where(fresh, 0.0, row_tile(states, p, h, span))
                        for p in range(pole_count)
                    )

                    def step(t, state):
                        u = row_tile(u_rows, t, h, span)
                        state = tuple(s * a + u for s, a in zip(state, decay))
                        terms = [s * g for s, g in zip(state, gain)]
                        while len(terms) > 1:
                            terms = [x + y for x, y in zip(terms[::2], terms[1::2])]
                        y_rows[row_at(t, h, span), :] = terms[0]
                        return state

                    state = token_loop(lo, hi, step, state)
                    for p in range(pole_count):
                        states[row_at(p, h, span), :] = state[p]
                    return 0

                lax.fori_loop(0, halves, half, 0)

            return start + length

        lax.fori_loop(0, request_count, request, jnp.int32(0))

        def block(b, _):
            rows = pl.ds(pl.multiple_of(c * CHUNK + b * SUBS, SUBS), SUBS)
            for j in range(tiles):
                lanes = slice(j * LANES, (j + 1) * LANES)
                index = pl.ds(b * SUBS * span + j, SUBS, stride=span)
                out_buf[rows, lanes] = y_rows[index, :] + skip_ref[:, lanes] * u_rows[index, :]
            return 0

        lax.fori_loop(0, CHUNK // SUBS, block, 0)
        for copy in chunk_copies(((out_buf, out_hbm),), out_sems, c):
            copy.start()
        return 0

    lax.fori_loop(0, chunks, chunk, 0)
    for c in range(chunks):
        for copy in chunk_copies(((out_buf, out_hbm),), out_sems, c):
            copy.wait()


def scaled_rows(rate_ref, residue_ref, r_rows, tiles):
    pole_count = rate_ref.shape[0]
    span = max(tiles, SUBS)
    for pt in range(pole_count // SUBS):
        for j in range(tiles):
            rows = slice(pt * SUBS, (pt + 1) * SUBS)
            lanes = slice(j * LANES, (j + 1) * LANES)
            scaled = residue_ref[rows, lanes] * jnp.sqrt(
                1.0 - jnp.exp(-2.0 * rate_ref[rows, lanes])
            )
            r_rows[pl.ds(pt * SUBS * span + j, SUBS, stride=span), :] = scaled


def finish_kernel(
    request_count,
    hop_count,
    lengths_ref,
    w_hbm,
    q_hbm,
    rate_ref,
    residue_ref,
    *rest,
):
    hop_refs = rest[:hop_count]
    out_hbm, w_buf, q_buf, out_buf, y_rows, a_rows, z_rows, sems, out_sems = rest[hop_count:]
    i = lax.axis_index("ctx")
    pole_count, channels = rate_ref.shape
    tok_dev = w_buf.shape[0]
    tiles = channels // LANES
    span = max(tiles, SUBS)
    halves = span // SUBS
    chunks = tok_dev // CHUNK
    first = i * tok_dev
    moves = ((w_hbm, w_buf), (q_hbm, q_buf))
    for c in range(chunks):
        for copy in chunk_copies(moves, sems, c):
            copy.start()
    before = request_at(lengths_ref, first - 1, request_count)
    behind = request_at(lengths_ref, first - tok_dev - 1, request_count)
    _, end = request_span(lengths_ref, before, request_count)
    live = jnp.where(before < 0, 0, jnp.clip(end + 1 - first, 0, tok_dev))
    passed = (before >= 0) & (before == behind)
    to_rows(rate_ref, a_rows, tiles, lambda x: jnp.exp(-x))
    for pt in range(pole_count // SUBS):
        for j in range(tiles):
            rows = slice(pt * SUBS, (pt + 1) * SUBS)
            lanes = slice(j * LANES, (j + 1) * LANES)
            rate = rate_ref[rows, lanes]
            scaled = residue_ref[rows, lanes] * jnp.sqrt(1.0 - jnp.exp(-2.0 * rate))
            incoming = hop_refs[0][rows, lanes]
            for ref in hop_refs[1:]:
                incoming = incoming + jnp.where(passed, ref[rows, lanes], 0.0)
            z_rows[pl.ds(pt * SUBS * span + j, SUBS, stride=span), :] = (
                incoming * scaled * jnp.exp(-rate)
            )

    def chunk(c, _):
        for copy in chunk_copies(moves, sems, c):
            copy.wait()
        hi = jnp.clip(live - c * CHUNK, 0, CHUNK)

        @pl.when(hi > 0)
        def _():
            def half(h, _):
                decay = [row_tile(a_rows, p, h, span) for p in range(pole_count)]
                state = tuple(row_tile(z_rows, p, h, span) for p in range(pole_count))

                def step(t, state):
                    terms = list(state)
                    while len(terms) > 1:
                        terms = [x + y for x, y in zip(terms[::2], terms[1::2])]
                    y_rows[row_at(t, h, span), :] = terms[0]
                    return tuple(s * a for s, a in zip(state, decay))

                state = token_loop(jnp.int32(0), hi, step, state)
                for p in range(pole_count):
                    z_rows[row_at(p, h, span), :] = state[p]
                return 0

            lax.fori_loop(0, halves, half, 0)

        @pl.when(hi < CHUNK)
        def _():
            def zero(t, _):
                for h in range(halves):
                    y_rows[row_at(t, h, span), :] = jnp.zeros((SUBS, LANES), jnp.float32)
                return 0

            lax.fori_loop(hi, CHUNK, zero, 0)

        def block(b, _):
            rows = pl.ds(pl.multiple_of(c * CHUNK + b * 16, 16), 16)
            for j in range(tiles):
                lanes = slice(j * LANES, (j + 1) * LANES)
                y = jnp.concatenate(
                    [
                        y_rows[pl.ds((b * 16 + half * SUBS) * span + j, SUBS, stride=span), :]
                        for half in range(2)
                    ],
                    axis=0,
                )
                out_buf[rows, lanes] = (
                    q_buf[rows, lanes].astype(jnp.float32) * (w_buf[rows, lanes] + y)
                ).astype(jnp.bfloat16)
            return 0

        lax.fori_loop(0, CHUNK // 16, block, 0)
        for copy in chunk_copies(((out_buf, out_hbm),), out_sems, c):
            copy.start()
        return 0

    lax.fori_loop(0, chunks, chunk, 0)
    for c in range(chunks):
        for copy in chunk_copies(((out_buf, out_hbm),), out_sems, c):
            copy.wait()


SMEM = pl.BlockSpec(memory_space=pltpu.SMEM)
VMEM = pl.BlockSpec(memory_space=pltpu.VMEM)
ANY = pl.BlockSpec(memory_space=pl.ANY)


def params():
    return pltpu.CompilerParams(vmem_limit_bytes=VMEM_BYTES)


def swap_pairs(block, odd):
    n = lax.axis_size("ctx")
    route = [(i, (i + 1) % n if i % 2 == odd else (i - 1) % n) for i in range(n)]
    return lax.ppermute(block, "ctx", route)


def shards(q_feat, k_feat, v_feat, pole_rate, residue, skip_gain, lengths, owners):
    tok_dev, channels = q_feat.shape
    pole_count = pole_rate.shape[0]
    request_count = lengths.shape[0]
    n = lax.axis_size("ctx")
    i = lax.axis_index("ctx")
    rows = max(channels // LANES, SUBS)
    chunks = tok_dev // CHUNK
    longest = n * tok_dev // 2
    hops = max(2, -(-(longest - 1) // tok_dev))
    f32 = jnp.float32
    state_shape = jax.ShapeDtypeStruct((pole_count, channels), f32)
    far_count = n - 3
    element = tok_dev * channels * pole_count
    pieces = pl.pallas_call(
        functools.partial(pieces_kernel, request_count),
        out_shape=[state_shape] * (4 + far_count),
        in_specs=[SMEM, SMEM, ANY, ANY, VMEM],
        out_specs=[VMEM] * (4 + far_count),
        scratch_shapes=[
            pltpu.VMEM((tok_dev, channels), jnp.bfloat16),
            pltpu.VMEM((tok_dev, channels), jnp.bfloat16),
            pltpu.VMEM((CHUNK * rows, LANES), f32),
            pltpu.VMEM((pole_count * rows, LANES), f32),
            pltpu.VMEM((request_count * pole_count * rows, LANES), f32),
            pltpu.SemaphoreType.DMA((2, chunks)),
        ],
        compiler_params=params(),
        cost_estimate=pl.CostEstimate(
            flops=2 * element, bytes_accessed=4 * tok_dev * channels, transcendentals=0
        ),
        name="pieces",
    )(lengths, owners, k_feat, v_feat, pole_rate)
    even_out, odd_out, next_out, own = pieces[:4]
    is_odd = (i % 2) == 1
    even_in = swap_pairs(even_out, 0)
    odd_in = swap_pairs(odd_out, 1)
    far = [
        lax.ppermute(block, "ctx", [(j, (j + 2 + d) % n) for j in range(n)])
        for d, block in enumerate(pieces[4:])
    ]

    local = pl.pallas_call(
        functools.partial(local_kernel, request_count),
        out_shape=jax.ShapeDtypeStruct((tok_dev, channels), f32),
        in_specs=[SMEM, ANY, ANY, VMEM, VMEM, VMEM],
        out_specs=ANY,
        scratch_shapes=[
            pltpu.VMEM((tok_dev, channels), jnp.bfloat16),
            pltpu.VMEM((tok_dev, channels), jnp.bfloat16),
            pltpu.VMEM((tok_dev, channels), f32),
            pltpu.VMEM((CHUNK * rows, LANES), f32),
            pltpu.VMEM((CHUNK * rows, LANES), f32),
            pltpu.VMEM((pole_count * rows, LANES), f32),
            pltpu.VMEM((pole_count * rows, LANES), f32),
            pltpu.VMEM((pole_count * rows, LANES), f32),
            pltpu.SemaphoreType.DMA((2, chunks)),
            pltpu.SemaphoreType.DMA((1, chunks)),
        ],
        compiler_params=params(),
        cost_estimate=pl.CostEstimate(
            flops=4 * element, bytes_accessed=8 * tok_dev * channels, transcendentals=0
        ),
        name="local",
    )(lengths, k_feat, v_feat, pole_rate, residue, skip_gain[None, :])

    starts = jnp.cumsum(lengths) - lengths
    ends = starts + lengths - 1
    first = i * tok_dev
    before = jnp.sum((starts <= first - 1).astype(jnp.int32)) - 1
    behind = jnp.sum((starts <= first - tok_dev - 1).astype(jnp.int32)) - 1
    at_last = jnp.sum((starts <= first + tok_dev - 1).astype(jnp.int32)) - 1
    passing = at_last == before
    passed = (before == behind) & (before >= 0)

    from_behind = jnp.where(is_odd, even_in, odd_in)
    from_ahead = jnp.where(is_odd, odd_in, even_in)
    arrived = [from_behind]
    block = next_out
    span = jnp.exp(-pole_rate * tok_dev)
    for hop in range(1, hops):
        prior = arrived[-1] if hop == 1 else jnp.where(passed, arrived[-1], 0.0)
        block = jnp.where(passing, span * prior, next_out if hop == 1 else 0.0)
        even_hop, odd_hop = swap_pairs(block, 0), swap_pairs(block, 1)
        arrived.append(jnp.where(is_odd, even_hop, odd_hop))

    mixed_out = pl.pallas_call(
        functools.partial(finish_kernel, request_count, hops),
        out_shape=jax.ShapeDtypeStruct((tok_dev, channels), jnp.bfloat16),
        in_specs=[SMEM, ANY, ANY, VMEM, VMEM] + [VMEM] * hops,
        out_specs=ANY,
        scratch_shapes=[
            pltpu.VMEM((tok_dev, channels), f32),
            pltpu.VMEM((tok_dev, channels), jnp.bfloat16),
            pltpu.VMEM((tok_dev, channels), jnp.bfloat16),
            pltpu.VMEM((CHUNK * rows, LANES), f32),
            pltpu.VMEM((pole_count * rows, LANES), f32),
            pltpu.VMEM((pole_count * rows, LANES), f32),
            pltpu.SemaphoreType.DMA((2, chunks)),
            pltpu.SemaphoreType.DMA((1, chunks)),
        ],
        compiler_params=params(),
        cost_estimate=pl.CostEstimate(
            flops=2 * element, bytes_accessed=8 * tok_dev * channels, transcendentals=0
        ),
        name="finish",
    )(lengths, local, q_feat, pole_rate, residue, *arrived)

    owner_before = jnp.sum(jnp.where(jnp.arange(request_count) == before, owners, 0))
    end_before = jnp.sum(jnp.where(jnp.arange(request_count) == before, ends, 0))
    reach = jnp.maximum(end_before - (first - 1), 0).astype(f32)
    mine = passed & (owner_before == i)
    carried = jnp.where(mine, jnp.exp(-pole_rate * reach) * from_behind, 0.0)
    decode_state = own + from_ahead + sum(far)
    decode_state = decode_state + jnp.where(i == 0, from_behind, carried)
    decode_state = decode_state + jnp.where(passed | (i == 0), 0.0, arrived[1])
    return mixed_out, decode_state[None]


def solution(mesh):
    placed = (
        P(("groups", "ctx"), "chan"),
        P(("groups", "ctx"), "chan"),
        P(("groups", "ctx"), "chan"),
        P(None, "chan"),
        P(None, "chan"),
        P("chan"),
        P("groups"),
        P("groups"),
    )
    return jax.shard_map(
        shards,
        mesh=mesh,
        in_specs=placed,
        out_specs=(P(("groups", "ctx"), "chan"), P(("groups", "ctx"), None, "chan")),
        check_vma=False,
    )
```

time: 432 us -> 64.8 us (0.15)
  matrix products: 167 us -> 0 us
  other arithmetic: 141 us -> 3.59 us
  local copies, waits for them, and re-layouts: 64.3 us -> 7 us
  Pallas kernels: 0 us -> 31.9 us
  loops' own time: 27.7 us -> 0 us
  starting transfers between devices: 19.4 us -> 13.4 us
    dot_general x34 -> x0, matrix products: 167 us -> none  [the longest x16 110 us: block_step(): jnp.einsum('ts,tsc,sc->tc', same_seg, toeplitz, u_block, precision=HIGH)]
    dot_general x32 -> x0, other arithmetic: 58 us -> none  [the longest x16 46.1 us: block_step(): jnp.einsum('psc,sc->pc', decay_back, weighted, precision=HIGH)]
    pallas_call x0 -> x3, Pallas kernels: none -> 31.9 us  [the longest x1 16.1 us: shards(): pl.pallas_call(functools.partial(local_kernel, request_count), out_shape=...]
    convert_element_type x52 -> x0, other arithmetic: 30.3 us -> none  [the longest x16 11.2 us: block_step(): live_mask = (seg_block == carry_seg).astype(jnp.float32)]
    another operation x2 -> x0, loops' own time: 27.7 us -> none  [the longest x1 27.6 us: shards(): lax.scan(block_step, init_carry, block_inputs)]
    while x32 -> x0, other arithmetic: 18 us -> none
    dynamic_update_slice x16 -> x0, other arithmetic: 13.3 us -> none  [shards(): lax.scan(block_step, init_carry, block_inputs)]
    exp x1 -> x0, local copies, waits for them, and re-layouts: 12.6 us -> none  [shards(): jnp.exp(-pole_rate[:, None, :] * (step_float[None, :, None] + 1.0))]
  transfers between devices with their start and end apart: 4 -> 5, of which waited for: 3 -> 1; matrix products, arithmetic and copies ran while one was open for 14% -> 4% of each run, Pallas kernels for 0% -> 25%
where the time goes in v1:
time: 64.8 us
  Pallas kernels  31.9 us (49%)
  starting transfers between devices  13.4 us (21%)
  local copies, waits for them, and re-layouts  7 us (11%)
  waiting for transfers between devices  4.81 us (7%)
  between operations  4.08 us (6%)
  other arithmetic  3.59 us (6%)
    pallas_call x1, Pallas kernels, shards(): pl.pallas_call(functools.partial(local_kernel, request_count), out_shape=...  16.1 us
    ppermute x4, starting transfers between devices, swap_pairs(): return lax.ppermute(block, 'ctx', route)  13.2 us
    pallas_call x1, Pallas kernels, shards(): pl.pallas_call(functools.partial(pieces_kernel, request_count), out_shape...  9.19 us
    unnamed x28, local copies, waits for them, and re-layouts  7 us
    pallas_call x1, Pallas kernels, shards(): pl.pallas_call(functools.partial(finish_kernel, request_count, hops), out...  6.58 us
    ppermute x4, waiting for transfers between devices, swap_pairs(): return lax.ppermute(block, 'ctx', route)  4.81 us
  transfers between devices with their start and end apart: 5, of which 1 were waited for; matrix products, arithmetic and copies ran while one was open for 4% of the time, Pallas kernels for 25%

profile of v1, /device:TPU:0, one launch (start us, length us, event | category | flops | bytes accessed | tf_op | source)
XLA Modules:
  0.0 64.8 jit_solution(5517692255327253231)
XLA Ops:
  0.6 0.0 copy-start
  0.6 1.6 %copy-done = bf16[512,2048]{1,0:T(8,128)(2,1)S(1)} copy-done((bf16[512,2048]{1,0:T(8,128)(2,1)S(1)}, bf16[512,2048]{1,0:T(8,128)(2,1)}, u32[]{:S(2)}) %copy-start) | copy-done | bytes 2097176
  2.2 1.6 %copy-done.2 = bf16[512,2048]{1,0:T(8,128)(2,1)S(1)} copy-done((bf16[512,2048]{1,0:T(8,128)(2,1)S(1)}, bf16[512,2048]{1,0:T(8,128)(2,1)}, u32[]{:S(2)}) %copy-start.2) | copy-done | bytes 2097176
  3.8 0.9 %copy-done.4 = f32[16,2048]{1,0:T(8,128)S(1)} copy-done((f32[16,2048]{1,0:T(8,128)S(1)}, f32[16,2048]{1,0:T(8,128)}, u32[]{:S(2)}) %copy-start.4) | copy-done | bytes 131096
  4.7 0.7 %copy-done.9 = s32[4]{0:T(128)S(1)} copy-done((s32[4]{0:T(128)S(1)}, s32[4]{0:T(128)}, u32[]{:S(2)}) %copy-start.9) | copy-done | bytes 40
  5.4 0.7 %copy-done.11 = s32[4]{0:T(128)S(1)} copy-done((s32[4]{0:T(128)S(1)}, s32[4]{0:T(128)}, u32[]{:S(2)}) %copy-start.11) | copy-done | bytes 40
  6.0 0.0 copy-start.7
  6.1 0.0 copy-start.8
  6.1 9.2 %pieces.1 = (f32[16,2048]{1,0:T(8,128)S(1)}, f32[16,2048]{1,0:T(8,128)S(1)}, f32[16,2048]{1,0:T(8,128)S(1)}, f32[16,2048]{1,0:T(8,128)S(1)}, f32[16,2048]{1,0:T(8,128)S(1)}) custom-call(s32[4]{0:T(128)S(1)} %copy-done.9, s32[4]{0:T(128)S(1)} %copy-done.11, bf16[512,2048]{1,0:T(8,128)(2,1)S(1)} %copy-done, bf16[512,2048]{1,0:T(8,128)(2,1)S(1)} %copy-done.2, ...), custom_call_target="tpu_custom_call" | custom-call | flops 33554432 | bytes 4194304 | tf_op jit(solution)/shard_map/pieces/pallas_call | solution.py:440
  15.3 3.1 %collective-permute-start = (f32[16,2048]{1,0:T(8,128)S(1)}, f32[16,2048]{1,0:T(8,128)S(1)}, u32[]{:S(2)}, u32[]{:S(2)}) collective-permute-start(f32[16,2048]{1,0:T(8,128)S(1)} %get-tuple-element.7), channel_id=1, source_target_pairs={{0,4},{4,0},{8,12},{12,8},{1,5},{5,1},{9,13},{13,9},{2,6},{6,2},{1... | collective-permute-start | bytes 393224 | tf_op jit(solution)/shard_map/ppermute | solution.py:423
  18.3 2.4 %collective-permute-start.1 = (f32[16,2048]{1,0:T(8,128)S(1)}, f32[16,2048]{1,0:T(8,128)S(1)}, u32[]{:S(2)}, u32[]{:S(2)}) collective-permute-start(f32[16,2048]{1,0:T(8,128)S(1)} %get-tuple-element.8), channel_id=1, source_target_pairs={{0,12},{4,8},{8,4},{12,0},{1,13},{5,9},{9,5},{13,1},{2,14},{6,10},... | collective-permute-start | bytes 393224 | tf_op jit(solution)/shard_map/ppermute | solution.py:423
  20.8 0.2 collective-permute-start.4
  20.9 0.0 copy-done.10
  20.9 0.2 reduce-window.9
  21.1 0.7 %fusion.4 = (s32[]{:T(128)}, s32[]{:T(128)}, s32[]{:T(128)}) fusion(s32[]{:T(128)S(6)} %sub.34, s32[4]{0:T(128)S(1)} %copy-done.10, s32[4,1]{0,1:T(1,128)S(1)} %reduce-window.9, s32[]{:T(128)S(6)} %sub.32, s32[]{:T(128)S(6)} %sub.30), kind=kLoop, calls=%fused_computation.13 | loop fusion | flops 37 | bytes 56 | tf_op jit(solution)/shard_map/reduce_sum | solution.py:496
  23.2 0.0 collective-permute-done
  23.2 4.8 %collective-permute-done.1 = f32[16,2048]{1,0:T(8,128)S(1)} collective-permute-done((f32[16,2048]{1,0:T(8,128)S(1)}, f32[16,2048]{1,0:T(8,128)S(1)}, u32[]{:S(2)}, u32[]{:S(2)}) %collective-permute-start.1) | collective-permute-done | bytes 131104 | tf_op jit(solution)/shard_map/ppermute | solution.py:423
  28.0 0.0 copy-done.13
  28.0 0.0 copy-done.5
  28.1 1.1 %collective-permute-start.3 = (f32[16,2048]{1,0:T(8,128)S(1)}, f32[16,2048]{1,0:T(8,128)S(1)}, u32[]{:S(2)}, u32[]{:S(2)}) collective-permute-start(f32[16,2048]{1,0:T(8,128)S(1)} %get-tuple-element.17), channel_id=1, source_target_pairs={{0,12},{4,8},{8,4},{12,0},{1,13},{5,9},{9,5},{13,1},{2,14},{6,10},... | collective-permute-start | bytes 393224 | tf_op jit(solution)/shard_map/ppermute | solution.py:423
  29.2 6.6 %collective-permute-start.2 = (f32[16,2048]{1,0:T(8,128)S(1)}, f32[16,2048]{1,0:T(8,128)S(1)}, u32[]{:S(2)}, u32[]{:S(2)}) collective-permute-start(f32[16,2048]{1,0:T(8,128)S(1)} %get-tuple-element.17), channel_id=1, source_target_pairs={{0,4},{4,0},{8,12},{12,8},{1,5},{5,1},{9,13},{13,9},{2,6},{6,2},{1... | collective-permute-start | bytes 393224 | tf_op jit(solution)/shard_map/ppermute | solution.py:423
  35.8 1.2 %fusion.1 = s32[]{:T(128)} fusion(s32[4,1]{0,1:T(1,128)} %copy-done.13, s32[]{:T(128)S(6)} %sub.33), kind=kLoop, calls=%fused_computation.10 | loop fusion | flops 15 | bytes 24 | tf_op jit(solution)/shard_map/reduce_sum | solution.py:535
  37.7 0.0 copy-done.12
  37.7 0.6 fusion
  39.7 0.0 copy-start.3
  39.7 1.6 %copy-done.3 = bf16[512,2048]{1,0:T(8,128)(2,1)S(1)} copy-done((bf16[512,2048]{1,0:T(8,128)(2,1)S(1)}, bf16[512,2048]{1,0:T(8,128)(2,1)}, u32[]{:S(2)}) %copy-start.3) | copy-done | bytes 2097176
  41.3 16.1 %local.1.w_hbm = f32[512,2048]{1,0:T(8,128)S(1)} custom-call(s32[4]{0:T(128)S(1)} %copy-done.10, bf16[512,2048]{1,0:T(8,128)(2,1)S(1)} %copy-done.1, bf16[512,2048]{1,0:T(8,128)(2,1)S(1)} %copy-done.3, f32[16,2048]{1,0:T(8,128)S(1)} %copy-done.5, f32[16,2048]{1,0:T(8,128)S(1)} %copy-done.7, f32[1,2048]{1,0:T(1,128)S(1)} %bitcast.15), custom_call_target="tpu_custom_call" | custom-call | flops 67108864 | bytes 8388608 | tf_op jit(solution)/shard_map/local/pallas_call | solution.py:468
  57.4 0.0 collective-permute-done.4
  57.4 0.0 collective-permute-done.3
  57.4 0.0 collective-permute-done.2
  57.4 0.8 %add_bitcast_fusion = (f32[1,16,2048]{2,1,0:T(8,128)}, f32[16,2048]{1,0:T(8,128)S(1)}) fusion(f32[16,2048]{1,0:T(8,128)S(1)} %get-tuple-element.18.rest_0_, f32[16,2048]{1,0:T(8,128)S(1)} %collective-permute-done.4, f32[16,2048]{1,0:T(8,128)S(1)} %get-tuple-element.10, f32[16,2048]{1,0:T(8,128)S(1)} %collective-permute-done.1, ...), kind=kLoop, calls=%fused_computation | loop fusion | flops 393216 | bytes 1310728 | tf_op jit(solution)/shard_map/broadcast_in_dim | solution.py:542
  58.2 6.6 %finish.1 = bf16[512,2048]{1,0:T(8,128)(2,1)} custom-call(s32[4]{0:T(128)S(1)} %copy-done.10, f32[512,2048]{1,0:T(8,128)S(1)} %local.1.w_hbm, bf16[512,2048]{1,0:T(8,128)(2,1)S(1)} %copy-done.6, f32[16,2048]{1,0:T(8,128)S(1)} %copy-done.5, f32[16,2048]{1,0:T(8,128)S(1)} %copy-done.7, f32[16,2048]{1,0:T(8,128)S(1)} %get-tuple-element.18.rest_0_, ...), custom_call_target="tpu_custom_call" | custom-call | flops 33554432 | bytes 8388608 | tf_op jit(solution)/shard_map/finish/pallas_call | solution.py:512
  (15 shorter events, 0.1 us)
Async XLA Ops:
  0.6 1.6 %copy-start = (bf16[512,2048]{1,0:T(8,128)(2,1)S(1)}, bf16[512,2048]{1,0:T(8,128)(2,1)}, u32[]{:S(2)}) copy-start(bf16[512,2048]{1,0:T(8,128)(2,1)} %k_hbm.3) | copy-start | bytes 6291460
  2.2 1.6 %copy-start.2 = (bf16[512,2048]{1,0:T(8,128)(2,1)S(1)}, bf16[512,2048]{1,0:T(8,128)(2,1)}, u32[]{:S(2)}) copy-start(bf16[512,2048]{1,0:T(8,128)(2,1)} %v_hbm.3) | copy-start | bytes 6291460
  3.8 0.9 %copy-start.4 = (f32[16,2048]{1,0:T(8,128)S(1)}, f32[16,2048]{1,0:T(8,128)}, u32[]{:S(2)}) copy-start(f32[16,2048]{1,0:T(8,128)} %rate_ref.5) | copy-start | bytes 393220
  4.7 0.7 %copy-start.9 = (s32[4]{0:T(128)S(1)}, s32[4]{0:T(128)}, u32[]{:S(2)}) copy-start(s32[4]{0:T(128)} %lengths_ref.5) | copy-start | bytes 52
  5.4 0.7 %copy-start.11 = (s32[4]{0:T(128)S(1)}, s32[4]{0:T(128)}, u32[]{:S(2)}) copy-start(s32[4]{0:T(128)} %owners_ref.1) | copy-start | bytes 52
  6.0 14.9 %copy-start.10 = (s32[4]{0:T(128)S(1)}, s32[4]{0:T(128)}, u32[]{:S(2)}) copy-start(s32[4]{0:T(128)} %lengths_ref.5) | copy-start | bytes 52
  6.0 22.0 %copy-start.5 = (f32[16,2048]{1,0:T(8,128)S(1)}, f32[16,2048]{1,0:T(8,128)}, u32[]{:S(2)}) copy-start(f32[16,2048]{1,0:T(8,128)} %rate_ref.5) | copy-start | bytes 393220
  6.0 31.6 %copy-start.12 = (s32[4]{0:T(128)S(1)}, s32[4]{0:T(128)}, u32[]{:S(2)}) copy-start(s32[4]{0:T(128)} %owners_ref.1) | copy-start | bytes 52
  6.0 33.6 %copy-start.1 = (bf16[512,2048]{1,0:T(8,128)(2,1)S(1)}, bf16[512,2048]{1,0:T(8,128)(2,1)}, u32[]{:S(2)}) copy-start(bf16[512,2048]{1,0:T(8,128)(2,1)} %k_hbm.3) | copy-start | bytes 6291460
  6.0 33.6 %copy-start.7 = (f32[16,2048]{1,0:T(8,128)S(1)}, f32[16,2048]{1,0:T(8,128)}, u32[]{:S(2)}) copy-start(f32[16,2048]{1,0:T(8,128)} %residue_ref.3) | copy-start | bytes 393220
  6.1 33.6 %copy-start.8 = (f32[2048]{0:T(1024)S(1)}, f32[2048]{0:T(1024)}, u32[]{:S(2)}) copy-start(f32[2048]{0:T(1024)} %param.13) | copy-start | bytes 24580
  15.3 8.0 %collective-permute-start = (f32[16,2048]{1,0:T(8,128)S(1)}, f32[16,2048]{1,0:T(8,128)S(1)}, u32[]{:S(2)}, u32[]{:S(2)}) collective-permute-start(f32[16,2048]{1,0:T(8,128)S(1)} %get-tuple-element.7), channel_id=1, source_target_pairs={{0,4},{4,0},{8,12},{12,8},{1,5},{5,1},{9,13},{13,9},{2,6},{6,2},{1... | collective-permute-start | bytes 393224 | tf_op jit(solution)/shard_map/ppermute | solution.py:423
  18.3 9.7 %collective-permute-start.1 = (f32[16,2048]{1,0:T(8,128)S(1)}, f32[16,2048]{1,0:T(8,128)S(1)}, u32[]{:S(2)}, u32[]{:S(2)}) collective-permute-start(f32[16,2048]{1,0:T(8,128)S(1)} %get-tuple-element.8), channel_id=1, source_target_pairs={{0,12},{4,8},{8,4},{12,0},{1,13},{5,9},{9,5},{13,1},{2,14},{6,10},... | collective-permute-start | bytes 393224 | tf_op jit(solution)/shard_map/ppermute | solution.py:423
  20.8 36.6 %collective-permute-start.4 = (f32[16,2048]{1,0:T(8,128)S(1)}, f32[16,2048]{1,0:T(8,128)S(1)}, u32[]{:S(2)}, u32[]{:S(2)}) collective-permute-start(f32[16,2048]{1,0:T(8,128)S(1)} %get-tuple-element.11), channel_id=1, source_target_pairs={{0,8},{4,12},{8,0},{12,4},{1,9},{5,13},{9,1},{13,5},{2,10},{6,14},... | collective-permute-start | bytes 393224 | tf_op jit(solution)/shard_map/ppermute | solution.py:464
  21.1 6.9 %copy-start.13 = (s32[4,1]{0,1:T(1,128)}, s32[4,1]{0,1:T(1,128)S(1)}, u32[]{:S(2)}) copy-start(s32[4,1]{0,1:T(1,128)S(1)} %reduce-window.9) | copy-start | bytes 52
  28.1 29.3 %collective-permute-start.3 = (f32[16,2048]{1,0:T(8,128)S(1)}, f32[16,2048]{1,0:T(8,128)S(1)}, u32[]{:S(2)}, u32[]{:S(2)}) collective-permute-start(f32[16,2048]{1,0:T(8,128)S(1)} %get-tuple-element.17), channel_id=1, source_target_pairs={{0,12},{4,8},{8,4},{12,0},{1,13},{5,9},{9,5},{13,1},{2,14},{6,10},... | collective-permute-start | bytes 393224 | tf_op jit(solution)/shard_map/ppermute | solution.py:423
  29.2 28.2 %collective-permute-start.2 = (f32[16,2048]{1,0:T(8,128)S(1)}, f32[16,2048]{1,0:T(8,128)S(1)}, u32[]{:S(2)}, u32[]{:S(2)}) collective-permute-start(f32[16,2048]{1,0:T(8,128)S(1)} %get-tuple-element.17), channel_id=1, source_target_pairs={{0,4},{4,0},{8,12},{12,8},{1,5},{5,1},{9,13},{13,9},{2,6},{6,2},{1... | collective-permute-start | bytes 393224 | tf_op jit(solution)/shard_map/ppermute | solution.py:423
  39.7 1.6 %copy-start.3 = (bf16[512,2048]{1,0:T(8,128)(2,1)S(1)}, bf16[512,2048]{1,0:T(8,128)(2,1)}, u32[]{:S(2)}) copy-start(bf16[512,2048]{1,0:T(8,128)(2,1)} %v_hbm.3) | copy-start | bytes 6291460
  41.3 16.9 %copy-start.6 = (bf16[512,2048]{1,0:T(8,128)(2,1)S(1)}, bf16[512,2048]{1,0:T(8,128)(2,1)}, u32[]{:S(2)}) copy-start(bf16[512,2048]{1,0:T(8,128)(2,1)} %q_hbm.1) | copy-start | bytes 6291460
